TPU v7x, 512 devices: a whole 4x4x16 slice. The times are simulated.
512 devices in a mesh: grp: 16 (over y, x), node: 32 (over z, core).
Axes of the slice: x: 4, y: 4, z: 16, core: 2. Of those that a mesh axis runs over, the one named last changes fastest.
Arguments:
- damage: bfloat16 [4096, 65536], P('grp', 'node'), may hold values from -6 to 6
- basis_table: bfloat16 [4096, 512], P('grp'), may hold values from -6 to 6
- train_ids: int32 [4096], P('grp'), may hold values from 0 to 4095, each once
- counts: int32 [16], replicated, may hold values from 64 to 256
- new_table: bfloat16 [2048, 512], replicated, may hold values from -6 to 6
- new_ids: int32 [1024], replicated, may hold values from 0 to 2047
Outputs:
- surrogate: bfloat16 [1024, 65536], P('grp', 'node')
- peak: float32 [1024], P('grp')
- spread: float32 [1024], P('grp')
Inputs may be any that keep to these rules, and one draw needn't show every extreme that they name: `train_ids`: each row of basis_table is named by exactly one slot.
All inputs are finite; a program needn't handle non-finite values.
Results may differ from a plain program's by a relative error of at most 0.0085.
Values may be sent and summed in bfloat16 or wider, within the bound.
A program may use at most 64 MiB of HBM per device.

v0:
```python
import jax
import jax.numpy as jnp
from jax import lax
from jax.sharding import PartitionSpec as P


def cut_along(value, dim, size):
    before, after = (value.shape[:dim], value.shape[dim + 1 :])
    return jnp.moveaxis(value.reshape(*before, size, -1, *after), dim, 0)


def sent_and_summed(value, axis, dim):
    blocks = cut_along(value, dim, lax.axis_size(axis))
    arrived = lax.all_to_all(blocks, axis, split_axis=0, concat_axis=0, tiled=True)
    return arrived.astype(jnp.float32).sum(axis=0)


def from_everyone(value, axis):
    size = lax.axis_size(axis)
    return lax.all_to_all(
        jnp.broadcast_to(value[None], (size, *value.shape)), axis, 0, 0, tiled=True
    )


def in_order(blocks, dim):
    dims = list(blocks.shape[1:])
    dims[dim] *= blocks.shape[0]
    return jnp.moveaxis(blocks, 0, dim).reshape(dims)


def gather_directly(value, axis, dim):
    blocks = from_everyone(value, axis)
    return in_order(blocks, dim)


def collected_together(value, axis):
    leaves = jax.tree.leaves(value)
    sequence = sorted(range(len(leaves)), key=lambda k: -leaves[k].size)
    width = (1, *leaves[sequence[0]].shape)[-1]
    lines = [
        jnp.pad(leaves[k].reshape(-1), (0, -leaves[k].size % width)).reshape(-1, width)
        for k in sequence
    ]
    both, at, found = (from_everyone(jnp.concatenate(lines), axis), 0, {})
    for k, line in zip(sequence, lines):
        section = both[:, at : at + len(line)].reshape(len(both), -1)
        found[k] = section[:, : leaves[k].size].reshape(-1, *leaves[k].shape)
        at += len(line)
    numbers = iter(range(len(leaves)))
    return jax.tree.map(lambda _: found[next(numbers)], value)


def folded_in_pairs(pieces, combine):
    while len(jax.tree.leaves(pieces)[0]) > 1:
        pieces = jax.vmap(combine)(
            *(jax.tree.map(lambda part: part[side::2], pieces) for side in (0, 1))
        )
    return jax.tree.map(lambda part: part[0], pieces)


def joined_all(value, axis, combine):
    pieces = collected_together(value, axis)
    return folded_in_pairs(pieces, combine)


def combine_stats(first, second):
    return (first[0] + second[0], jnp.maximum(first[1], second[1]))


def local(damage, basis_table, train_ids, counts, new_table, new_ids):
    slot_count = damage.shape[0]
    node_cells = damage.shape[1]
    group_index = lax.axis_index("grp")
    group_total = lax.axis_size("grp")
    total_nodes = node_cells * lax.axis_size("node")
    per_group = new_ids.shape[0] // group_total
    sample_total = jnp.sum(counts).astype(jnp.float32)
    basis_whole, ids_whole = (
        lax.all_gather(basis_table, "grp", axis=0, tiled=True),
        lax.all_gather(train_ids, "grp", axis=0, tiled=True),
    )
    my_slot_ids = lax.dynamic_slice_in_dim(ids_whole, group_index * slot_count, slot_count, 0)
    live_slot = jnp.arange(slot_count, dtype=jnp.int32) < counts[group_index]
    chosen = jnp.take(basis_whole, my_slot_ids, axis=0)
    weighted = jnp.where(live_slot[:, None], chosen, jnp.zeros_like(chosen))
    my_ids = lax.dynamic_slice_in_dim(new_ids, group_index * per_group, per_group, 0)
    new_rows = jnp.take(new_table, my_ids, axis=0)
    term_cols = weighted
    product = lax.dot_general(
        term_cols, damage, (((0,), (0,)), ((), ())), preferred_element_type=jnp.float32
    )
    coef_share = sent_and_summed((product / sample_total).astype(jnp.bfloat16), "grp", 0)
    term_cols = new_rows
    values = jnp.dot(
        term_cols,
        gather_directly(coef_share.astype(jnp.bfloat16), "grp", 0),
        preferred_element_type=jnp.float32,
    )
    local_square = jnp.sum(values * values, axis=1)
    local_peak = jnp.max(values, axis=1)
    squares, peak_value = joined_all((local_square, local_peak), "node", combine_stats)
    surrogate = values.astype(jnp.bfloat16)
    spread = jnp.sqrt(squares / total_nodes + 1e-06)
    return (surrogate, peak_value, spread)


def solution(mesh):
    placed = (P("grp", "node"), P("grp", None), P("grp"), P(), P(), P())
    return jax.shard_map(
        local,
        mesh=mesh,
        in_specs=placed,
        out_specs=(P("grp", "node"), P("grp"), P("grp")),
        check_vma=False,
    )
```

profile of v0, /device:TPU:1, one launch (start us, length us, event | category | flops | bytes accessed | tf_op | source)
XLA Modules:
  0.0 196.4 jit_solution(9732886169708049763)
XLA Ops:
  7.2 0.0 copy-start
  7.2 0.0 copy-start.1
  7.2 0.0 all-gather.3.cloned.1.call-start
  7.2 0.7 all-gather.3.cloned.1.call-update
  7.9 1.3 reduce_sum.30
  9.2 1.2 dynamic_slice.10
  11.1 19.1 %all-gather = s32[16,1,256]{2,1,0:T(1,128)S(1)} all-gather(s32[1,1,256]{2,1,0:T(1,128)} %bitcast.23), channel_id=1, replica_groups=mesh['grp'=16,'node'=32] {'grp'}, dimensions={0}, use_global_device_ids=true | all-gather | bytes 17408 | tf_op jit(solution)/shard_map/all_gather | solution.py:80
  30.2 0.7 compare_and_fusion
  30.9 52.3 %all-gather.3.cloned.1.call-done = bf16[4096,512]{1,0:T(8,128)(2,1)} async-done(((bf16[256,512]{1,0:T(8,128)(2,1)}), bf16[4096,512]{1,0:T(8,128)(2,1)}) %all-gather.3.cloned.1.call-update) | async-done | bytes 4194320 | tf_op jit(solution)/shard_map/all_gather | solution.py:79
  83.2 3.9 %gather_fusion.1 = bf16[256,512]{1,0:T(8,128)(2,1)S(1)} fusion(bf16[4096,512]{1,0:T(8,128)(2,1)} %all-gather.3.cloned.1.call-done, s32[1024]{0:T(1024)S(1)} %pad_clamp_fusion), kind=kCustom, calls=%fused_computation.1 | custom fusion | bytes 525312 | tf_op jit(solution)/shard_map/jit(_take)/gather | solution.py:84
  87.2 0.0 copy-done.1
  87.2 0.9 divide_convert_fusion
  88.0 32.2 %all_to_all.15 = bf16[16,32,2048]{2,1,0:T(8,128)(2,1)} all-to-all(bf16[16,32,2048]{2,1,0:T(8,128)(2,1)S(1)} %bitcast.15), channel_id=1, replica_groups=mesh['grp'=16,'node'=32] {'grp'}, dimensions={0} | all-to-all | bytes 4194304 | tf_op jit(solution)/shard_map/all_to_all | solution.py:14
  120.3 2.0 %reduce_sum.31 = bf16[32,2048]{1,0:T(8,128)(2,1)S(1)} reduce(bf16[16,32,2048]{2,1,0:T(8,128)(2,1)} %all_to_all.15, bf16[]{:T(256)} %constant.53.clone.1), dimensions={0}, to_apply=%region_1.2 | reduce | flops 983040 | bytes 2228226 | tf_op jit(solution)/shard_map/reduce_sum | solution.py:15
  122.3 1.6 broadcast_in_dim.56
  123.8 4.4 %all-to-all-start.1 = ((bf16[16,32,2048]{2,1,0:T(8,128)(2,1)}), bf16[16,32,2048]{2,1,0:T(8,128)(2,1)}, u32[]{:S(2)}, u32[]{:S(2)}) async-start(bf16[16,32,2048]{2,1,0:T(8,128)(2,1)} %broadcast_in_dim.56), calls=%async_computation.1 | async-start | bytes 4194304 | tf_op jit(solution)/shard_map/all_to_all | solution.py:20
  128.2 0.8 compare_and_fusion.1
  129.0 0.0 copy-done
  129.0 0.7 gather_fusion
  129.7 25.8 %all-to-all-done.1 = bf16[16,32,2048]{2,1,0:T(8,128)(2,1)} async-done(((bf16[16,32,2048]{2,1,0:T(8,128)(2,1)}), bf16[16,32,2048]{2,1,0:T(8,128)(2,1)}, u32[]{:S(2)}, u32[]{:S(2)}) %all-to-all-start.1) | async-done | bytes 2097184 | tf_op jit(solution)/shard_map/all_to_all | solution.py:20
  155.5 2.9 %multiply_reduce_fusion = (f32[64]{0:T(128)S(1)}, f32[64]{0:T(128)S(1)}, bf16[64,2048]{1,0:T(8,128)(2,1)}) fusion(bf16[512,2048]{1,0:T(8,128)(2,1)} %bitcast.4, bf16[64,512]{1,0:T(8,128)(2,1)S(1)} %gather_fusion, pred[64]{0:T(512)(128)(4,1)S(1)} %get-tuple-element.5), kind=kOutput, calls=%fused_computation.3 | convolution fusion | flops 134774656 | bytes 2425408 | tf_op jit(solution)/shard_map/dot_general | solution.py:94
  158.5 0.1 reshape.71
  158.6 28.3 %all_to_all.16 = f32[32,1,128]{2,1,0:T(1,128)S(1)} all-to-all(f32[32,1,128]{2,1,0:T(1,128)S(1)} %reshape.71), channel_id=1, replica_groups=mesh['grp'=16,'node'=32] {'node'}, dimensions={0} | all-to-all | bytes 32768 | tf_op jit(solution)/shard_map/all_to_all | solution.py:20
  186.8 0.5 broadcast.26
  187.3 0.7 reduce.1
  188.0 0.1 reshape.72
  188.5 0.5 sqrt_bitcast_fusion
  189.0 0.5 maximum_bitcast_fusion
  (29 shorter events, 0.4 us)
Async XLA Ops:
  7.2 121.9 %copy-start = (bf16[2048,512]{1,0:T(8,128)(2,1)S(1)}, bf16[2048,512]{1,0:T(8,128)(2,1)}, u32[]{:S(2)}) copy-start(bf16[2048,512]{1,0:T(8,128)(2,1)} %param.10) | copy-start | bytes 6291460
  7.2 80.0 %copy-start.1 = (bf16[256,2048]{1,0:T(8,128)(2,1)S(1)}, bf16[256,2048]{1,0:T(8,128)(2,1)}, u32[]{:S(2)}) copy-start(bf16[256,2048]{1,0:T(8,128)(2,1)} %param.6) | copy-start | bytes 3145732
  7.2 76.0 %all-gather.3.cloned.1.call-start = ((), (), s32[]{:S(2)}) async-start(), calls=%async_computation.3 | async-start | bytes 4456448 | tf_op jit(solution)/shard_map/all_gather | solution.py:79
  123.8 31.7 %all-to-all-start.1 = ((bf16[16,32,2048]{2,1,0:T(8,128)(2,1)}), bf16[16,32,2048]{2,1,0:T(8,128)(2,1)}, u32[]{:S(2)}, u32[]{:S(2)}) async-start(bf16[16,32,2048]{2,1,0:T(8,128)(2,1)} %broadcast_in_dim.56), calls=%async_computation.1 | async-start | bytes 4194304 | tf_op jit(solution)/shard_map/all_to_all | solution.py:20
Sparse Core Ops, SparseCore 0:
  11.0 72.1 all-gather.2
where the time goes:
time: 197 us; the launch traced here: 196 us
  blocking collectives  79.6 us (40%)
  waiting for transfers between devices  78.7 us (40%)
  between operations  14.8 us (8%)
  local copies, waits for them, and re-layouts  8.48 us (4%)
  other arithmetic  6.56 us (3%)
  starting transfers between devices  4.46 us (2%)
  matrix products  3.8 us (2%)
    all_gather x1, waiting for transfers between devices, local(): lax.all_gather(basis_table, 'grp', axis=0, tiled=True)  52.3 us
    all_to_all x1, blocking collectives, sent_and_summed(): lax.all_to_all(blocks, axis, split_axis=0, concat_axis=0, tiled=True)  32.2 us
    all_to_all x1, blocking collectives, from_everyone(): lax.all_to_all(jnp.broadcast_to(value[None], (size, *value.shape)), axis,...  28.3 us
    all_to_all x1, waiting for transfers between devices, from_everyone(): lax.all_to_all(jnp.broadcast_to(value[None], (size, *value.shape)), axis,...  25.8 us
    all_gather x1, blocking collectives, local(): lax.all_gather(train_ids, 'grp', axis=0, tiled=True)  19.1 us
    all_to_all x1, starting transfers between devices, from_everyone(): lax.all_to_all(jnp.broadcast_to(value[None], (size, *value.shape)), axis,...  4.42 us
  transfers between devices with their start and end apart: 2, of which 2 were waited for; matrix products, arithmetic and copies ran while one was open for 2% of the time, Pallas kernels for 0%

commit v1 on v0

--- a/solution.py
+++ b/solution.py
@@ -76,7 +76,9 @@
     per_group = new_ids.shape[0] // group_total
     sample_total = jnp.sum(counts).astype(jnp.float32)
     basis_whole, ids_whole = (
-        lax.all_gather(basis_table, "grp", axis=0, tiled=True),
+        jnp.concatenate(
+            lax.all_to_all(jnp.stack([basis_table] * lax.axis_size("grp")), "grp", 0, 0), axis=0
+        ),
         lax.all_gather(train_ids, "grp", axis=0, tiled=True),
     )
     my_slot_ids = lax.dynamic_slice_in_dim(ids_whole, group_index * slot_count, slot_count, 0)

time: 197 us -> 188 us (0.954)
  waiting for transfers between devices: 78.7 us -> 21.6 us
  blocking collectives: 79.6 us -> 132 us
  between operations: 14.8 us -> 1.44 us
  starting transfers between devices: 4.46 us -> 12.2 us
  local copies, waits for them, and re-layouts: 8.48 us -> 11.3 us
    all_gather x1 -> x0, waiting for transfers between devices: 52.3 us -> none  [local(): lax.all_gather(basis_table, 'grp', axis=0, tiled=True)]
    all_gather x1, blocking collectives: 19.1 us -> 63.8 us  [local(): lax.all_gather(train_ids, 'grp', axis=0, tiled=True)]
    all_to_all x1, blocking collectives: 28.3 us -> 42.2 us  [from_everyone(): lax.all_to_all(jnp.broadcast_to(value[None], (size, *value.shape)), axis,...]
    all_to_all x0 -> x1, starting transfers between devices: none -> 7.77 us  [local(): lax.all_to_all(jnp.stack([basis_table] * lax.axis_size('grp')), 'grp', 0, 0)]
    all_to_all x1, blocking collectives: 32.2 us -> 25.6 us  [sent_and_summed(): lax.all_to_all(blocks, axis, split_axis=0, concat_axis=0, tiled=True)]
    all_to_all x1, waiting for transfers between devices: 25.8 us -> 21.6 us  [from_everyone(): lax.all_to_all(jnp.broadcast_to(value[None], (size, *value.shape)), axis,...]
    another operation x0 -> x1, local copies, waits for them, and re-layouts: none -> 3.47 us  [local(): jnp.stack([basis_table] * lax.axis_size('grp'))]
  transfers between devices with their start and end apart: 2 -> 2, of which waited for: 2 -> 1; matrix products, arithmetic and copies ran while one was open for 2% -> 2% of each run, Pallas kernels for 0% -> 0%
where the time goes in v1:
time: 188 us
  blocking collectives  132 us (70%)
  waiting for transfers between devices  21.6 us (11%)
  starting transfers between devices  12.2 us (6%)
  local copies, waits for them, and re-layouts  11.3 us (6%)
  other arithmetic  5.9 us (3%)
  matrix products  3.8 us (2%)
    all_gather x1, blocking collectives, local(): lax.all_gather(train_ids, 'grp', axis=0, tiled=True)  63.8 us
    all_to_all x1, blocking collectives, from_everyone(): lax.all_to_all(jnp.broadcast_to(value[None], (size, *value.shape)), axis,...  42.2 us
    all_to_all x1, blocking collectives, sent_and_summed(): lax.all_to_all(blocks, axis, split_axis=0, concat_axis=0, tiled=True)  25.6 us
    all_to_all x1, waiting for transfers between devices, from_everyone(): lax.all_to_all(jnp.broadcast_to(value[None], (size, *value.shape)), axis,...  21.6 us
    all_to_all x1, starting transfers between devices, local(): lax.all_to_all(jnp.stack([basis_table] * lax.axis_size('grp')), 'grp', 0, 0)  7.77 us
    all_to_all x1, starting transfers between devices, from_everyone(): lax.all_to_all(jnp.broadcast_to(value[None], (size, *value.shape)), axis,...  4.42 us
    gather x1, local copies, waits for them, and re-layouts, local(): chosen = jnp.take(basis_whole, my_slot_ids, axis=0)  3.94 us
  transfers between devices with their start and end apart: 2, of which 1 were waited for; matrix products, arithmetic and copies ran while one was open for 2% of the time, Pallas kernels for 0%

profile of v1, /device:TPU:1, one launch (start us, length us, event | category | flops | bytes accessed | tf_op | source)
XLA Modules:
  0.0 187.9 jit_solution(4517727958809750916)
XLA Ops:
  0.6 0.0 copy-start
  0.6 3.5 %stack.2 = bf16[16,256,512]{2,1,0:T(8,128)(2,1)} broadcast(bf16[256,512]{1,0:T(8,128)(2,1)} %param.7), dimensions={1,2} | broadcast | bytes 4456448 | tf_op jit(solution)/shard_map/stack | solution.py:80
  4.1 0.0 copy-start.3
  4.1 0.0 copy-start.1
  4.1 7.8 %all-to-all-start = ((bf16[16,256,512]{2,1,0:T(8,128)(2,1)}), bf16[16,256,512]{2,1,0:T(8,128)(2,1)}, u32[]{:S(2)}, u32[]{:S(2)}) async-start(bf16[16,256,512]{2,1,0:T(8,128)(2,1)} %stack.2), calls=%async_computation | async-start | bytes 8388608 | tf_op jit(solution)/shard_map/all_to_all | solution.py:80
  11.9 0.0 copy-start.2
  11.9 0.0 copy-done.3
  11.9 0.6 reduce_sum.30
  13.2 0.6 dynamic_slice.10
  13.8 0.0 copy-done.1
  13.8 63.8 %all-gather = s32[16,1,256]{2,1,0:T(1,128)S(1)} all-gather(s32[1,1,256]{2,1,0:T(1,128)S(1)} %bitcast.24), channel_id=1, replica_groups=mesh['grp'=16,'node'=32] {'grp'}, dimensions={0}, use_global_device_ids=true | all-gather | bytes 17408 | tf_op jit(solution)/shard_map/all_gather | solution.py:82
  77.7 0.7 compare_and_fusion
  78.4 0.0 all-to-all-done
  78.4 3.9 %gather_fusion.1 = bf16[256,512]{1,0:T(8,128)(2,1)S(1)} fusion(bf16[4096,512]{1,0:T(8,128)(2,1)} %bitcast.3, s32[1024]{0:T(1024)S(1)} %pad_clamp_fusion), kind=kCustom, calls=%fused_computation.1 | custom fusion | bytes 525312 | tf_op jit(solution)/shard_map/jit(_take)/gather | solution.py:86
  82.3 0.0 copy-done.2
  82.3 0.9 divide_convert_fusion
  83.2 25.6 %all_to_all.20 = bf16[16,32,2048]{2,1,0:T(8,128)(2,1)} all-to-all(bf16[16,32,2048]{2,1,0:T(8,128)(2,1)S(1)} %bitcast.16), channel_id=1, replica_groups=mesh['grp'=16,'node'=32] {'grp'}, dimensions={0} | all-to-all | bytes 4194304 | tf_op jit(solution)/shard_map/all_to_all | solution.py:14
  108.9 2.0 %reduce_sum.31 = bf16[32,2048]{1,0:T(8,128)(2,1)S(1)} reduce(bf16[16,32,2048]{2,1,0:T(8,128)(2,1)} %all_to_all.20, bf16[]{:T(256)} %constant.53.clone.1), dimensions={0}, to_apply=%region_1.2 | reduce | flops 983040 | bytes 2228226 | tf_op jit(solution)/shard_map/reduce_sum | solution.py:15
  110.9 1.6 broadcast_in_dim.56
  112.4 4.4 %all-to-all-start.2 = ((bf16[16,32,2048]{2,1,0:T(8,128)(2,1)}), bf16[16,32,2048]{2,1,0:T(8,128)(2,1)}, u32[]{:S(2)}, u32[]{:S(2)}) async-start(bf16[16,32,2048]{2,1,0:T(8,128)(2,1)} %broadcast_in_dim.56), calls=%async_computation.2 | async-start | bytes 4194304 | tf_op jit(solution)/shard_map/all_to_all | solution.py:20
  116.8 0.8 compare_and_fusion.1
  117.6 0.0 copy-done
  117.6 0.7 gather_fusion
  118.3 21.6 %all-to-all-done.2 = bf16[16,32,2048]{2,1,0:T(8,128)(2,1)} async-done(((bf16[16,32,2048]{2,1,0:T(8,128)(2,1)}), bf16[16,32,2048]{2,1,0:T(8,128)(2,1)}, u32[]{:S(2)}, u32[]{:S(2)}) %all-to-all-start.2) | async-done | bytes 2097184 | tf_op jit(solution)/shard_map/all_to_all | solution.py:20
  139.9 2.9 %multiply_reduce_fusion = (f32[64]{0:T(128)S(1)}, f32[64]{0:T(128)S(1)}, bf16[64,2048]{1,0:T(8,128)(2,1)}) fusion(bf16[512,2048]{1,0:T(8,128)(2,1)} %bitcast.5, bf16[64,512]{1,0:T(8,128)(2,1)S(1)} %gather_fusion, pred[64]{0:T(512)(128)(4,1)S(1)} %get-tuple-element.5), kind=kOutput, calls=%fused_computation.3 | convolution fusion | flops 134774656 | bytes 2425408 | tf_op jit(solution)/shard_map/dot_general | solution.py:96
  142.9 0.1 reshape.77
  143.0 42.2 %all_to_all.21 = f32[32,1,128]{2,1,0:T(1,128)S(1)} all-to-all(f32[32,1,128]{2,1,0:T(1,128)S(1)} %reshape.77), channel_id=1, replica_groups=mesh['grp'=16,'node'=32] {'node'}, dimensions={0} | all-to-all | bytes 32768 | tf_op jit(solution)/shard_map/all_to_all | solution.py:20
  185.2 0.5 broadcast.28
  185.7 0.7 reduce.1
  186.4 0.1 reshape.78
  186.9 0.5 maximum_bitcast_fusion
  187.4 0.5 sqrt_bitcast_fusion
  (29 shorter events, 0.4 us)
Async XLA Ops:
  0.6 117.0 %copy-start = (bf16[2048,512]{1,0:T(8,128)(2,1)S(1)}, bf16[2048,512]{1,0:T(8,128)(2,1)}, u32[]{:S(2)}) copy-start(bf16[2048,512]{1,0:T(8,128)(2,1)} %param.10) | copy-start | bytes 6291460
  4.1 7.8 %copy-start.3 = (s32[16]{0:T(128)S(1)}, s32[16]{0:T(128)}, u32[]{:S(2)}) copy-start(s32[16]{0:T(128)} %param.9) | copy-start | bytes 196
  4.1 9.7 %copy-start.1 = (s32[256]{0:T(256)S(1)}, s32[256]{0:T(256)}, u32[]{:S(2)}) copy-start(s32[256]{0:T(256)} %param.8) | copy-start | bytes 3076
  4.1 74.3 %all-to-all-start = ((bf16[16,256,512]{2,1,0:T(8,128)(2,1)}), bf16[16,256,512]{2,1,0:T(8,128)(2,1)}, u32[]{:S(2)}, u32[]{:S(2)}) async-start(bf16[16,256,512]{2,1,0:T(8,128)(2,1)} %stack.2), calls=%async_computation | async-start | bytes 8388608 | tf_op jit(solution)/shard_map/all_to_all | solution.py:80
  11.9 70.4 %copy-start.2 = (bf16[256,2048]{1,0:T(8,128)(2,1)S(1)}, bf16[256,2048]{1,0:T(8,128)(2,1)}, u32[]{:S(2)}) copy-start(bf16[256,2048]{1,0:T(8,128)(2,1)} %param.6) | copy-start | bytes 3145732
  112.4 27.5 %all-to-all-start.2 = ((bf16[16,32,2048]{2,1,0:T(8,128)(2,1)}), bf16[16,32,2048]{2,1,0:T(8,128)(2,1)}, u32[]{:S(2)}, u32[]{:S(2)}) async-start(bf16[16,32,2048]{2,1,0:T(8,128)(2,1)} %broadcast_in_dim.56), calls=%async_computation.2 | async-start | bytes 4194304 | tf_op jit(solution)/shard_map/all_to_all | solution.py:20
